TPU v7x, 32 devices: a whole 2x2x4 slice. The times are simulated.
32 devices in a mesh: groups: 2 (over y), dec: 16 (over z, x, core).
Axes of the slice: x: 2, y: 2, z: 4, core: 2. Of those that a mesh axis runs over, the one named last changes fastest.
Arguments:
- panels: bfloat16 [512, 64, 512], P(('groups', 'dec')), parts along dimension 0, may hold values from -6 to 6
- tile_panels: int32 [128, 16], P(('groups', 'dec')), parts along dimension 0, may hold values from 0 to 255, as said below
- tile_count: int32 [32], P(('groups', 'dec')), parts along dimension 0, may hold values from 1 to 4, as said below
- conv_weight: bfloat16 [3, 3, 3, 512, 256], replicated, may hold values from -0.0546875 to 0.0546875
- conv_bias: float32 [256], replicated, may hold values from -4 to 4
- norm_gain: float32 [256], replicated, may hold values from 0.1 to 1.9
- norm_shift: float32 [256], replicated, may hold values from -3 to 3
Outputs:
- decoded: bfloat16 [128, 392, 256], P(('groups', 'dec')), parts along dimension 0
There are 2 independent parts, one for each index of `groups`. A program takes and returns all parts, laid end to end along the dimension named above; an argument that names none is the same for every part. Nothing has to cross between parts.
Inputs may be any that keep to these rules, and one draw needn't show every extreme that they name: `tile_panels`: panel p lies on device p // 16. Over all 4 rows of one device, at most 4 entries name panels of any one device, repeats counted; in every draw each device's rows name exactly 4 panels on each of 16 devices. `tile_count`: in every draw some device has 4 live rows.
All inputs are finite; a program needn't handle non-finite values.
Results may differ from a plain program's by a relative error of at most 0.001.
Values may be sent and summed in bfloat16 or wider, within the bound.
A program may use at most 128 MiB of HBM per device.

v0:
```python
import jax
import jax.numpy as jnp
from jax import lax
from jax.sharding import PartitionSpec as P

C_OUT = 256
GROUPS = 32
PH = 8
PW = 8
GH = 2
GW = 2
WT = 4
OCELLS = 392


epsilon = 1e-06


def arrange_window(panel_rows, frame_count, grid_high, grid_wide, panel_high, panel_wide):
    channels = panel_rows.shape[-1]
    blocks = panel_rows.reshape(frame_count, grid_high, grid_wide, panel_high, panel_wide, channels)
    blocks = blocks.transpose(0, 1, 3, 2, 4, 5)
    return blocks.reshape(frame_count, grid_high * panel_high, grid_wide * panel_wide, channels)


def decode_window(window, kernel, conv_bias, norm_gain, norm_shift, groups):
    out_frames = window.shape[0] - 2
    out_high = window.shape[1] - 2
    out_wide = window.shape[2] - 2
    pieces = []
    for tap_t in range(3):
        for tap_h in range(3):
            for tap_w in range(3):
                pieces.append(
                    window[
                        tap_t : tap_t + out_frames,
                        tap_h : tap_h + out_high,
                        tap_w : tap_w + out_wide,
                        :,
                    ]
                )
    columns = jnp.concatenate(pieces, axis=-1)
    columns = columns.reshape(out_frames * out_high * out_wide, columns.shape[-1])
    conv_out = jnp.dot(columns, kernel, preferred_element_type=jnp.float32) + conv_bias
    cell_count = conv_out.shape[0]
    width_out = conv_out.shape[1]
    grouped = conv_out.reshape(cell_count, groups, width_out // groups)
    center = jnp.mean(grouped, axis=(0, 2), keepdims=True)
    shifted = grouped - center
    spread = jnp.mean(shifted * shifted, axis=(0, 2), keepdims=True)
    normed = (shifted / jnp.sqrt(spread + epsilon)).reshape(cell_count, width_out)
    scaled = normed * norm_gain + norm_shift
    return jax.nn.silu(scaled).astype(jnp.bfloat16)


def fetch_panels(panels, work_rows, live_tiles, capacity):
    devices = lax.axis_size("dec")
    per_device = panels.shape[0]
    tile_rows, slot_count = work_rows.shape
    wanted = work_rows.reshape(tile_rows * slot_count)
    ref_live = jnp.arange(tile_rows * slot_count, dtype=jnp.int32) // slot_count < live_tiles
    owner_dev = wanted // per_device
    local_row = wanted % per_device
    device_ids = jnp.arange(devices, dtype=jnp.int32)
    matches = ((owner_dev[:, None] == device_ids[None, :]) & ref_live[:, None]).astype(jnp.int32)
    before = jnp.cumsum(matches, axis=0) - matches
    slot_rank = jnp.sum(before * matches, axis=1)
    where_to = owner_dev * capacity + slot_rank
    target = jnp.where(ref_live, where_to, devices * capacity)
    request = jnp.full((devices * capacity,), -1, jnp.int32).at[target].set(local_row, mode="drop")
    asked_rows = lax.all_to_all(
        request.reshape(devices, capacity), "dec", split_axis=0, concat_axis=0, tiled=True
    )
    picked = panels[jnp.maximum(asked_rows, 0)]
    returned = lax.all_to_all(picked, "dec", split_axis=0, concat_axis=0, tiled=True)
    landed = returned.reshape(devices * capacity, panels.shape[1], panels.shape[2])
    chosen = landed[jnp.where(ref_live, where_to, 0)]
    return chosen.reshape(tile_rows, slot_count, panels.shape[1], panels.shape[2])


def body(panels, tile_panels, tile_count, conv_weight, conv_bias, norm_gain, norm_shift):
    devices = lax.axis_size("dec")
    tile_rows, slot_count = tile_panels.shape
    capacity = max(1, tile_rows * slot_count // devices)
    kernel = conv_weight.reshape(27 * conv_weight.shape[3], conv_weight.shape[4])
    own_count = tile_count[0]
    windows = fetch_panels(panels, tile_panels, own_count, capacity)

    def decode_into(work, buffer, source_row, dest_row):
        window = arrange_window(work[source_row], WT, GH, GW, PH, PW)
        tile_out = decode_window(window, kernel, conv_bias, norm_gain, norm_shift, GROUPS)
        return lax.dynamic_update_slice_in_dim(buffer, tile_out[None], dest_row, 0)

    results = jnp.zeros((tile_rows, OCELLS, C_OUT), jnp.bfloat16)
    decoded = lax.fori_loop(
        0, own_count, lambda step, buffer: decode_into(windows, buffer, step, step), results
    )
    return decoded


def solution(mesh):
    in_specs = (
        P(("groups", "dec"), None, None),
        P(("groups", "dec"), None),
        P(("groups", "dec")),
        P(),
        P(),
        P(),
        P(),
    )
    out_specs = P(("groups", "dec"), None, None)
    return jax.shard_map(body, mesh=mesh, in_specs=in_specs, out_specs=out_specs, check_vma=False)
```

profile of v0, /device:TPU:30, one launch (start us, length us, event | category | flops | bytes accessed | tf_op | source)
XLA Modules:
  0.0 315.4 jit_solution(12587733459709594561)
XLA Ops:
  3.6 8.1 %all_to_all.14 = s32[16,1,4]{2,1,0:T(1,128)S(1)} all-to-all(s32[16,1,4]{2,1,0:T(1,128)S(1)} %bitcast.65), channel_id=1, replica_groups=mesh['groups'=2,'dec'=16] {'dec'}, dimensions={0} | all-to-all | bytes 512 | tf_op jit(solution)/shard_map/all_to_all | solution.py:71
  11.9 2.7 gather_fusion
  14.6 8.5 %all-to-all-start.1 = ((bf16[16,4,64,512]{3,2,1,0:T(8,128)(2,1)}), bf16[16,4,64,512]{3,2,1,0:T(8,128)(2,1)}, u32[]{:S(2)}, u32[]{:S(2)}) async-start(bf16[16,4,64,512]{3,2,1,0:T(8,128)(2,1)} %bitcast.64), calls=%async_computation.1 | async-start | bytes 8388608 | tf_op jit(solution)/shard_map/all_to_all | solution.py:75
  23.1 91.3 %all-to-all-done.1 = bf16[16,4,64,512]{3,2,1,0:T(8,128)(2,1)} async-done(((bf16[16,4,64,512]{3,2,1,0:T(8,128)(2,1)}), bf16[16,4,64,512]{3,2,1,0:T(8,128)(2,1)}, u32[]{:S(2)}, u32[]{:S(2)}) %all-to-all-start.1) | async-done | bytes 4194336 | tf_op jit(solution)/shard_map/all_to_all | solution.py:75
  114.4 4.9 %gather_fusion.1 = bf16[64,64,512]{2,1,0:T(8,128)(2,1)} fusion(bf16[64,64,512]{2,1,0:T(8,128)(2,1)} %bitcast.9, s32[1024]{0:T(1024)S(1)} %pad_clamp_fusion), kind=kCustom, calls=%fused_computation.1 | custom fusion | bytes 8388864 | tf_op jit(solution)/shard_map/gather | solution.py:77
  119.5 195.0 %while.10 = (s32[]{:T(128)}, bf16[4,392,256]{2,1,0:T(8,128)(2,1)S(1)}, s32[]{:T(128)}, bf16[4,16,64,512]{3,2,1,0:T(8,128)(2,1)}, bf16[13824,256]{1,0:T(8,128)(2,...) while((s32[]{:T(128)}, ...), condition=%wide.region_8.9_spmd, body=%wide.region_3.8_spmd.sunk | while | flops 2775937024 | bytes 68437160 | solution.py:95
  120.1 1.3 constant_dynamic-slice_fusion.2
  137.0 1.0 slice_dynamic-update-slice_fusion.71
  139.7 1.0 slice_dynamic-update-slice_fusion.74
  146.2 12.5 %reshape.269 = bf16[392,13824]{1,0:T(8,128)(2,1)} reshape(bf16[2,14,14,13824]{3,2,1,0:T(8,128)(2,1)} %slice_dynamic-update-slice_fusion.80) | data formatting | bytes 21676032 | tf_op jit(solution)/shard_map/while/body/reshape | solution.py:43
  158.7 8.4 %fusion.15 = (f32[256]{0:T(256)S(1)}, f32[392,256]{1,0:T(8,128)S(1)}) fusion(f32[256]{0:T(256)S(1)} %get-tuple-element.154, bf16[392,13824]{1,0:T(8,128)(2,1)} %reshape.269, bf16[13824,256]{1,0:T(8,128)(2,1)} %get-tuple-element.153), kind=kOutput, calls=%fused_computation.71.clone.1 | convolution fusion | flops 2774732544 | bytes 18319360 | tf_op jit(solution)/shard_map/while/body/dot_general | solution.py:44
  168.7 1.3 constant_dynamic-slice_fusion.2
  185.6 1.0 slice_dynamic-update-slice_fusion.71
  194.7 12.5 %reshape.269 = bf16[392,13824]{1,0:T(8,128)(2,1)} reshape(bf16[2,14,14,13824]{3,2,1,0:T(8,128)(2,1)} %slice_dynamic-update-slice_fusion.80) | data formatting | bytes 21676032 | tf_op jit(solution)/shard_map/while/body/reshape | solution.py:43
  207.2 8.4 %fusion.15 = (f32[256]{0:T(256)S(1)}, f32[392,256]{1,0:T(8,128)S(1)}) fusion(f32[256]{0:T(256)S(1)} %get-tuple-element.154, bf16[392,13824]{1,0:T(8,128)(2,1)} %reshape.269, bf16[13824,256]{1,0:T(8,128)(2,1)} %get-tuple-element.153), kind=kOutput, calls=%fused_computation.71.clone.1 | convolution fusion | flops 2774732544 | bytes 18319360 | tf_op jit(solution)/shard_map/while/body/dot_general | solution.py:44
  217.3 1.3 constant_dynamic-slice_fusion.2
  234.2 1.0 slice_dynamic-update-slice_fusion.71
  243.3 12.5 %reshape.269 = bf16[392,13824]{1,0:T(8,128)(2,1)} reshape(bf16[2,14,14,13824]{3,2,1,0:T(8,128)(2,1)} %slice_dynamic-update-slice_fusion.80) | data formatting | bytes 21676032 | tf_op jit(solution)/shard_map/while/body/reshape | solution.py:43
  255.8 8.4 %fusion.15 = (f32[256]{0:T(256)S(1)}, f32[392,256]{1,0:T(8,128)S(1)}) fusion(f32[256]{0:T(256)S(1)} %get-tuple-element.154, bf16[392,13824]{1,0:T(8,128)(2,1)} %reshape.269, bf16[13824,256]{1,0:T(8,128)(2,1)} %get-tuple-element.153), kind=kOutput, calls=%fused_computation.71.clone.1 | convolution fusion | flops 2774732544 | bytes 18319360 | tf_op jit(solution)/shard_map/while/body/dot_general | solution.py:44
  265.9 1.3 constant_dynamic-slice_fusion.2
  282.7 1.0 slice_dynamic-update-slice_fusion.71
  285.5 1.0 slice_dynamic-update-slice_fusion.74
  291.9 12.5 %reshape.269 = bf16[392,13824]{1,0:T(8,128)(2,1)} reshape(bf16[2,14,14,13824]{3,2,1,0:T(8,128)(2,1)} %slice_dynamic-update-slice_fusion.80) | data formatting | bytes 21676032 | tf_op jit(solution)/shard_map/while/body/reshape | solution.py:43
  304.4 8.4 %fusion.15 = (f32[256]{0:T(256)S(1)}, f32[392,256]{1,0:T(8,128)S(1)}) fusion(f32[256]{0:T(256)S(1)} %get-tuple-element.154, bf16[392,13824]{1,0:T(8,128)(2,1)} %reshape.269, bf16[13824,256]{1,0:T(8,128)(2,1)} %get-tuple-element.153), kind=kOutput, calls=%fused_computation.71.clone.1 | convolution fusion | flops 2774732544 | bytes 18319360 | tf_op jit(solution)/shard_map/while/body/dot_general | solution.py:44
  (180 shorter events, 100.7 us)
Async XLA Ops:
  0.0 11.8 %copy-start = (bf16[16,64,512]{2,1,0:T(8,128)(2,1)S(1)}, bf16[16,64,512]{2,1,0:T(8,128)(2,1)}, u32[]{:S(2)}) copy-start(bf16[16,64,512]{2,1,0:T(8,128)(2,1)} %param.9) | copy-start | bytes 3145732
  11.9 107.6 %copy-start.2 = (f32[256]{0:T(256)S(1)}, f32[256]{0:T(256)}, u32[]{:S(2)}) copy-start(f32[256]{0:T(256)} %param.14) | copy-start | bytes 3076
  11.9 107.6 %copy-start.3 = (f32[256]{0:T(256)S(1)}, f32[256]{0:T(256)}, u32[]{:S(2)}) copy-start(f32[256]{0:T(256)} %param.15) | copy-start | bytes 3076
  11.9 107.6 %copy-start.4 = (f32[256]{0:T(256)S(1)}, f32[256]{0:T(256)}, u32[]{:S(2)}) copy-start(f32[256]{0:T(256)} %param.13) | copy-start | bytes 3076
  14.6 99.8 %all-to-all-start.1 = ((bf16[16,4,64,512]{3,2,1,0:T(8,128)(2,1)}), bf16[16,4,64,512]{3,2,1,0:T(8,128)(2,1)}, u32[]{:S(2)}, u32[]{:S(2)}) async-start(bf16[16,4,64,512]{3,2,1,0:T(8,128)(2,1)} %bitcast.64), calls=%async_computation.1 | async-start | bytes 8388608 | tf_op jit(solution)/shard_map/all_to_all | solution.py:75
  314.5 0.9 copy-start.1
where the time goes:
time: 317 us; the launch traced here: 315 us
  local copies, waits for them, and re-layouts  167 us (53%)
  waiting for transfers between devices  91.3 us (29%)
  matrix products  33.5 us (11%)
  starting transfers between devices  8.51 us (3%)
  blocking collectives  8.15 us (3%)
  loops' own time  3.6 us (1%)
    while x104, local copies, waits for them, and re-layouts  94.6 us
    all_to_all x1, waiting for transfers between devices, fetch_panels(): lax.all_to_all(picked, 'dec', split_axis=0, concat_axis=0, tiled=True)  91.3 us
    reshape x4, local copies, waits for them, and re-layouts, decode_window(): columns.reshape(out_frames * out_high * out_wide, columns.shape[-1])  50 us
    dot_general x4, matrix products, decode_window(): jnp.dot(columns, kernel, preferred_element_type=jnp.float32) + conv_bias  33.5 us
    all_to_all x1, starting transfers between devices, fetch_panels(): lax.all_to_all(picked, 'dec', split_axis=0, concat_axis=0, tiled=True)  8.51 us
    all_to_all x1, blocking collectives, fetch_panels(): lax.all_to_all(request.reshape(devices, capacity), 'dec', split_axis=0, c...  8.15 us
  transfers between devices with their start and end apart: 1, of which 1 were waited for; matrix products, arithmetic and copies ran while one was open for 0% of the time, Pallas kernels for 0%

commit v1 on v0

v1 whole, which is shorter than its diff:
```python
import jax
import jax.numpy as jnp
from jax import lax
from jax.experimental import pallas as pl
from jax.experimental.pallas import tpu as pltpu
from jax.sharding import PartitionSpec as P

C_OUT = 256
GROUPS = 32
PH = 8
PW = 8
GH = 2
GW = 2
WT = 4
OCELLS = 392
ROW = GW * PW
OH = GH * PH - 2
OW = GW * PW - 2
OF = WT - 2
MROWS = OF * OH * ROW

epsilon = 1e-06


def pick_kernel(rows, panels, out, sem):
    count = out.shape[0]
    for i in range(count):
        pltpu.make_async_copy(panels.at[rows[i]], out.at[i], sem).start()
    pltpu.make_async_copy(out, out, sem).wait()


def pick_rows(panels, rows):
    return pl.pallas_call(
        pick_kernel,
        out_shape=jax.ShapeDtypeStruct((rows.shape[0], *panels.shape[1:]), panels.dtype),
        grid_spec=pltpu.PrefetchScalarGridSpec(
            num_scalar_prefetch=1,
            grid=(1,),
            in_specs=[pl.BlockSpec(memory_space=pl.ANY)],
            out_specs=pl.BlockSpec(memory_space=pl.ANY),
            scratch_shapes=[pltpu.SemaphoreType.DMA],
        ),
    )(rows, panels)


def fetch_panels(panels, work_rows, live_tiles, capacity):
    devices = lax.axis_size("dec")
    per_device = panels.shape[0]
    tile_rows, slot_count = work_rows.shape
    wanted = work_rows.reshape(tile_rows * slot_count)
    ref_live = jnp.arange(tile_rows * slot_count, dtype=jnp.int32) // slot_count < live_tiles
    owner_dev = wanted // per_device
    local_row = wanted % per_device
    order = jnp.arange(tile_rows * slot_count, dtype=jnp.int32)
    earlier = (owner_dev[:, None] == owner_dev[None, :]) & (order[None, :] < order[:, None])
    slot_rank = jnp.sum(earlier.astype(jnp.int32), axis=1)
    where_to = owner_dev * capacity + slot_rank
    places = jnp.arange(devices * capacity, dtype=jnp.int32)
    here = (where_to[None, :] == places[:, None]) & ref_live[None, :]
    request = jnp.sum(jnp.where(here, local_row[None, :], 0), axis=1)
    asked_rows = lax.all_to_all(
        request.reshape(devices, capacity), "dec", split_axis=0, concat_axis=0, tiled=True
    )
    picked = pick_rows(panels, asked_rows.reshape(-1))
    picked = picked.reshape(devices, capacity, *panels.shape[1:])
    returned = lax.all_to_all(picked, "dec", split_axis=0, concat_axis=0, tiled=True)
    landed = returned.reshape(devices * capacity, panels.shape[1], panels.shape[2])
    return landed, jnp.where(ref_live, where_to, 0)


def decode_kernel(idx, count, panels, weight, bias, gain, shift, out, stage, win, cols, flat, sems):
    tile = pl.program_id(0)
    slots = stage.shape[1]
    live = count[0]

    def fetch(which, slot):
        for s in range(slots):
            pltpu.make_async_copy(
                panels.at[idx[which * slots + s]], stage.at[slot, s], sems.at[slot]
            ).start()

    @pl.when(tile == 0)
    def _():
        fetch(0, 0)

    @pl.when(tile + 1 < live)
    def _():
        fetch(tile + 1, (tile + 1) % 2)

    @pl.when(tile < live)
    def _():
        slot = tile % 2
        pltpu.make_async_copy(stage.at[slot], stage.at[slot], sems.at[slot]).wait()
        channels = stage.shape[3]
        for f in range(WT):
            for g in range(GH):
                halves = [
                    stage[slot, (f * GH + g) * GW + h].astype(jnp.float32).reshape(PH, PW, channels)
                    for h in range(GW)
                ]
                rows = jnp.concatenate(halves, axis=1).reshape(PH * ROW, channels)
                win[f, pl.ds(g * PH * ROW, PH * ROW), :] = rows.astype(jnp.bfloat16)
        for a in range(3):
            for b in range(3):
                for f in range(OF):
                    cols[pl.ds(f * OH * ROW, OH * ROW), pl.ds((a * 3 + b) * channels, channels)] = win[
                        f + a, pl.ds(b * ROW, OH * ROW), :
                    ]
        conv = jnp.dot(cols[...], weight[0], preferred_element_type=jnp.float32)
        for c in (1, 2):
            part = jnp.dot(cols[...], weight[c], preferred_element_type=jnp.float32)
            conv = conv + pltpu.roll(part, MROWS - c, 0)
        conv = conv + bias[...]
        column = lax.broadcasted_iota(jnp.int32, (MROWS, C_OUT), 0) % ROW
        valid = column < OW
        lane = lax.broadcasted_iota(jnp.int32, (C_OUT, C_OUT), 0) // (C_OUT // GROUPS)
        other = lax.broadcasted_iota(jnp.int32, (C_OUT, C_OUT), 1) // (C_OUT // GROUPS)
        same = jnp.where(lane == other, 1.0, 0.0).astype(jnp.float32)
        cells = OCELLS * (C_OUT // GROUPS)

        def group_mean(x):
            total = jnp.sum(jnp.where(valid, x, 0.0), axis=0, keepdims=True)
            total = jnp.broadcast_to(total, (8, C_OUT))
            total = jnp.dot(
                total, same, preferred_element_type=jnp.float32, precision=lax.Precision.HIGHEST
            )
            return total[0:1] * (1.0 / cells)

        shifted = conv - group_mean(conv)
        spread = group_mean(shifted * shifted)
        scaled = shifted * (gain[...] / jnp.sqrt(spread + epsilon)) + shift[...]
        value = scaled / (1.0 + jnp.exp(-scaled))
        for q in range(OF * OH):
            flat[pl.ds(q * OW, OW), :] = value[q * ROW : q * ROW + OW, :]
        out[0] = flat[...].astype(jnp.bfloat16)

    @pl.when(tile >= live)
    def _():
        out[...] = jnp.zeros_like(out)


def decode(panels, idx, count, weight, conv_bias, norm_gain, norm_shift, tiles, slots):
    channels = panels.shape[2]
    whole = lambda t, *_: (0, 0)
    spec = pltpu.PrefetchScalarGridSpec(
        num_scalar_prefetch=2,
        grid=(tiles,),
        in_specs=[
            pl.BlockSpec(memory_space=pl.ANY),
            pl.BlockSpec(weight.shape, lambda t, *_: (0, 0, 0), pipeline_mode=pl.Buffered(1)),
            pl.BlockSpec((1, C_OUT), whole),
            pl.BlockSpec((1, C_OUT), whole),
            pl.BlockSpec((1, C_OUT), whole),
        ],
        out_specs=pl.BlockSpec((1, OCELLS, C_OUT), lambda t, *_: (t, 0, 0)),
        scratch_shapes=[
            pltpu.VMEM((2, slots, PH * PW, channels), jnp.bfloat16),
            pltpu.VMEM((WT, GH * PH * ROW, channels), jnp.bfloat16),
            pltpu.VMEM((MROWS, 9 * channels), jnp.bfloat16),
            pltpu.VMEM((OCELLS, C_OUT), jnp.float32),
            pltpu.SemaphoreType.DMA((2,)),
        ],
    )
    return pl.pallas_call(
        decode_kernel,
        out_shape=jax.ShapeDtypeStruct((tiles, OCELLS, C_OUT), jnp.bfloat16),
        grid_spec=spec,
        compiler_params=pltpu.CompilerParams(vmem_limit_bytes=40 * 2**20),
    )(
        idx,
        count,
        panels,
        weight,
        conv_bias.reshape(1, C_OUT),
        norm_gain.reshape(1, C_OUT),
        norm_shift.reshape(1, C_OUT),
    )


def body(panels, tile_panels, tile_count, conv_weight, conv_bias, norm_gain, norm_shift):
    devices = lax.axis_size("dec")
    tiles, slots = tile_panels.shape
    channels = panels.shape[2]
    weight = conv_weight.transpose(2, 0, 1, 3, 4).reshape(3, 9 * channels, C_OUT)
    if devices <= 16:
        held = lax.all_gather(panels, "dec", axis=0, tiled=True)
        idx = tile_panels.reshape(-1)
    else:
        capacity = max(1, tiles * slots // devices)
        held, idx = fetch_panels(panels, tile_panels, tile_count[0], capacity)
    return decode(
        held, idx, tile_count, weight, conv_bias, norm_gain, norm_shift, tiles, slots
    )


def solution(mesh):
    in_specs = (
        P(("groups", "dec"), None, None),
        P(("groups", "dec"), None),
        P(("groups", "dec")),
        P(),
        P(),
        P(),
        P(),
    )
    out_specs = P(("groups", "dec"), None, None)
    return jax.shard_map(body, mesh=mesh, in_specs=in_specs, out_specs=out_specs, check_vma=False)
```

time: 317 us -> 170 us (0.54)
  the two profiles are of different devices: /device:TPU:30 before, /device:TPU:21 now
where the time goes in v1:
time: 170 us; the launch traced here: 167 us
  waiting for transfers between devices  122 us (72%)
  Pallas kernels  20.5 us (12%)
  between operations  14.1 us (8%)
  local copies, waits for them, and re-layouts  10.5 us (6%)
    all_gather x1, waiting for transfers between devices, body(): held = lax.all_gather(panels, 'dec', axis=0, tiled=True)  122 us
    pallas_call x1, Pallas kernels, decode(): pl.pallas_call(decode_kernel, out_shape=jax.ShapeDtypeStruct((tiles, OCEL...  20.5 us
    transpose x1, local copies, waits for them, and re-layouts, body(): conv_weight.transpose(2, 0, 1, 3, 4).reshape(3, 9 * channels, C_OUT)  6.72 us
  transfers between devices with their start and end apart: 1, of which 1 were waited for; matrix products, arithmetic and copies ran while one was open for 4% of the time, Pallas kernels for 0%

profile of v1, /device:TPU:21, one launch (start us, length us, event | category | flops | bytes accessed | tf_op | source)
XLA Modules:
  0.0 167.4 jit_solution(12083054316188956736)
XLA Ops:
  6.5 0.0 all-gather.2.cloned.1.call-start
  6.5 0.7 all-gather.2.cloned.1.call-update
  7.9 0.8 reshape.15.idx
  8.7 0.0 copy-start.1
  8.7 0.0 copy-start.2
  8.7 0.0 copy-start.3
  8.7 6.7 %copy.9 = bf16[3,3,3,512,256]{4,3,2,1,0:T(8,128)(2,1)} copy(bf16[3,3,3,512,256]{4,3,0,2,1:T(8,128)(2,1)} %bitcast.9) | data formatting | bytes 14155776 | tf_op jit(solution)/shard_map/transpose | solution.py:184
  15.4 121.6 %all-gather.2.cloned.1.call-done.panels = bf16[256,64,512]{2,1,0:T(8,128)(2,1)} async-done(((bf16[16,64,512]{2,1,0:T(8,128)(2,1)}), bf16[256,64,512]{2,1,0:T(8,128)(2,1)}) %all-gather.2.cloned.1.call-update) | async-done | bytes 16777232 | tf_op jit(solution)/shard_map/all_gather | solution.py:186
  137.0 0.0 copy-done.1
  137.0 0.0 copy-done.2
  137.0 0.0 copy-done.3
  137.0 0.0 copy-start
  137.0 3.0 %copy-done = bf16[3,3,3,512,256]{4,3,2,1,0:T(8,128)(2,1)S(1)} copy-done((bf16[3,3,3,512,256]{4,3,2,1,0:T(8,128)(2,1)S(1)}, bf16[3,3,3,512,256]{4,3,2,1,0:T(8,128)(2,1)}, u32[]{:S(2)}) %copy-start) | copy-done | bytes 7077912
  140.0 20.5 %shard_map.73 = bf16[4,392,256]{2,1,0:T(8,128)(2,1)} custom-call(s32[64]{0:T(128)S(1)} %reshape.15.idx, s32[1]{0:T(128)S(6)} %copy.10.count, bf16[256,64,512]{2,1,0:T(8,128)(2,1)} %all-gather.2.cloned.1.call-done.panels, bf16[3,4608,256]{2,1,0:T(8,128)(2,1)S(1)} %bitcast.5, f32[1,256]{1,0:T(1,128)S(1)} %bitcast.6, f32[1,256]{1,0:T(1,128)S(1)} %bitcast.7, ...), custom_call_target="tpu_custom_call" | custom-call | tf_op jit(solution)/shard_map/pallas_call | solution.py:164
Async XLA Ops:
  6.5 130.4 %all-gather.2.cloned.1.call-start = ((), (), s32[]{:S(2)}) async-start(), calls=%async_computation | async-start | bytes 17825792 | tf_op jit(solution)/shard_map/all_gather | solution.py:186
  8.7 128.3 %copy-start.1 = (f32[256]{0:T(256)S(1)}, f32[256]{0:T(256)}, u32[]{:S(2)}) copy-start(f32[256]{0:T(256)} %param.11) | copy-start | bytes 3076
  8.7 128.3 %copy-start.2 = (f32[256]{0:T(256)S(1)}, f32[256]{0:T(256)}, u32[]{:S(2)}) copy-start(f32[256]{0:T(256)} %param.12) | copy-start | bytes 3076
  8.7 128.3 %copy-start.3 = (f32[256]{0:T(256)S(1)}, f32[256]{0:T(256)}, u32[]{:S(2)}) copy-start(f32[256]{0:T(256)} %param.13) | copy-start | bytes 3076
  137.0 3.0 %copy-start = (bf16[3,3,3,512,256]{4,3,2,1,0:T(8,128)(2,1)S(1)}, bf16[3,3,3,512,256]{4,3,2,1,0:T(8,128)(2,1)}, u32[]{:S(2)}) copy-start(bf16[3,3,3,512,256]{4,3,2,1,0:T(8,128)(2,1)} %copy.9) | copy-start | bytes 21233668
Sparse Core Ops, SparseCore 0:
  9.5 127.4 all-gather.1

commit v2 on v1

--- a/solution.py
+++ b/solution.py
@@ -182,12 +182,8 @@
     tiles, slots = tile_panels.shape
     channels = panels.shape[2]
     weight = conv_weight.transpose(2, 0, 1, 3, 4).reshape(3, 9 * channels, C_OUT)
-    if devices <= 16:
-        held = lax.all_gather(panels, "dec", axis=0, tiled=True)
-        idx = tile_panels.reshape(-1)
-    else:
-        capacity = max(1, tiles * slots // devices)
-        held, idx = fetch_panels(panels, tile_panels, tile_count[0], capacity)
+    capacity = max(1, tiles * slots // devices)
+    held, idx = fetch_panels(panels, tile_panels, tile_count[0], capacity)
     return decode(
         held, idx, tile_count, weight, conv_bias, norm_gain, norm_shift, tiles, slots
     )

time: 170 us -> 266 us (1.56)
  the two profiles are of different devices: /device:TPU:21 before, /device:TPU:17 now
where the time goes in v2:
time: 266 us; the launch traced here: 265 us
  Pallas kernels  149 us (56%)
  waiting for transfers between devices  85.4 us (32%)
  local copies, waits for them, and re-layouts  11.7 us (4%)
  blocking collectives  10.1 us (4%)
  starting transfers between devices  7.04 us (3%)
    pallas_call x1, Pallas kernels, pick_rows(): pl.pallas_call(pick_kernel, out_shape=jax.ShapeDtypeStruct((rows.shape[0]...  129 us
    all_to_all x1, waiting for transfers between devices, fetch_panels(): lax.all_to_all(picked, 'dec', split_axis=0, concat_axis=0, tiled=True)  85.4 us
    pallas_call x1, Pallas kernels, decode(): pl.pallas_call(decode_kernel, out_shape=jax.ShapeDtypeStruct((tiles, OCEL...  20.6 us
    all_to_all x1, blocking collectives, fetch_panels(): lax.all_to_all(request.reshape(devices, capacity), 'dec', split_axis=0, c...  10.1 us
    all_to_all x1, starting transfers between devices, fetch_panels(): lax.all_to_all(picked, 'dec', split_axis=0, concat_axis=0, tiled=True)  7.04 us
    transpose x1, local copies, waits for them, and re-layouts, body(): conv_weight.transpose(2, 0, 1, 3, 4).reshape(3, 9 * channels, C_OUT)  6.7 us
  transfers between devices with their start and end apart: 1, of which 1 were waited for; matrix products, arithmetic and copies ran while one was open for 3% of the time, Pallas kernels for 0%

profile of v2, /device:TPU:17, one launch (start us, length us, event | category | flops | bytes accessed | tf_op | source)
XLA Modules:
  0.0 265.4 jit_solution(13191767806534714994)
XLA Ops:
  0.7 0.8 reshape.133
  1.4 0.2 convert_reduce_fusion
  1.6 0.1 select_reduce_fusion
  1.7 0.1 all_to_all.9
  1.8 10.1 %all_to_all.14 = s32[16,1,4]{2,1,0:T(1,128)S(1)} all-to-all(s32[16,1,4]{2,1,0:T(1,128)S(1)} %bitcast.17), channel_id=1, replica_groups=mesh['groups'=2,'dec'=16] {'dec'}, dimensions={0} | all-to-all | bytes 512 | tf_op jit(solution)/shard_map/all_to_all | solution.py:61
  11.9 0.5 broadcast.139
  12.4 0.7 reduce.3
  13.1 0.6 reshape.134.rows
  13.7 128.8 %shard_map.73 = bf16[64,64,512]{2,1,0:T(8,128)(2,1)} custom-call(s32[64]{0:T(128)} %reshape.134.rows, bf16[16,64,512]{2,1,0:T(8,128)(2,1)} %panels.1), custom_call_target="tpu_custom_call" | custom-call | tf_op jit(solution)/shard_map/pallas_call | solution.py:33
  142.5 7.0 %all-to-all-start.1 = ((bf16[16,4,64,512]{3,2,1,0:T(8,128)(2,1)}), bf16[16,4,64,512]{3,2,1,0:T(8,128)(2,1)}, u32[]{:S(2)}, u32[]{:S(2)}) async-start(bf16[16,4,64,512]{3,2,1,0:T(8,128)(2,1)} %bitcast.15), calls=%async_computation.1 | async-start | bytes 8388608 | tf_op jit(solution)/shard_map/all_to_all | solution.py:66
  149.6 0.0 copy-start.1
  149.6 0.0 copy-start.2
  149.6 0.0 copy-start.3
  149.6 6.7 %copy.13 = bf16[3,3,3,512,256]{4,3,2,1,0:T(8,128)(2,1)} copy(bf16[3,3,3,512,256]{4,3,0,2,1:T(8,128)(2,1)} %bitcast.16) | data formatting | bytes 14155776 | tf_op jit(solution)/shard_map/transpose | solution.py:184
  156.3 85.4 %all-to-all-done.1 = bf16[16,4,64,512]{3,2,1,0:T(8,128)(2,1)} async-done(((bf16[16,4,64,512]{3,2,1,0:T(8,128)(2,1)}), bf16[16,4,64,512]{3,2,1,0:T(8,128)(2,1)}, u32[]{:S(2)}, u32[]{:S(2)}) %all-to-all-start.1) | async-done | bytes 4194336 | tf_op jit(solution)/shard_map/all_to_all | solution.py:66
  241.7 0.0 copy-done.1
  241.7 0.0 copy-done.2
  241.7 0.0 copy-done.3
  241.8 0.0 copy-start
  241.8 3.0 %copy-done = bf16[3,3,3,512,256]{4,3,2,1,0:T(8,128)(2,1)S(1)} copy-done((bf16[3,3,3,512,256]{4,3,2,1,0:T(8,128)(2,1)S(1)}, bf16[3,3,3,512,256]{4,3,2,1,0:T(8,128)(2,1)}, u32[]{:S(2)}) %copy-start) | copy-done | bytes 7077912
  244.8 20.6 %shard_map.74 = bf16[4,392,256]{2,1,0:T(8,128)(2,1)} custom-call(s32[64]{0:T(128)S(1)} %get-tuple-element.5.idx, s32[1]{0:T(128)} %copy.14.count, bf16[64,64,512]{2,1,0:T(8,128)(2,1)} %bitcast.3.panels, bf16[3,4608,256]{2,1,0:T(8,128)(2,1)S(1)} %bitcast.11, f32[1,256]{1,0:T(1,128)S(1)} %bitcast.12, f32[1,256]{1,0:T(1,128)S(1)} %bitcast.13, f32[1,256]{1,0:T(1,128)S(1)} %bitcast.14), custom_call_target="tpu_custom_call" | custom-call | tf_op jit(solution)/shard_map/pallas_call | solution.py:164
  (3 shorter events, 0.0 us)
Async XLA Ops:
  142.5 99.2 %all-to-all-start.1 = ((bf16[16,4,64,512]{3,2,1,0:T(8,128)(2,1)}), bf16[16,4,64,512]{3,2,1,0:T(8,128)(2,1)}, u32[]{:S(2)}, u32[]{:S(2)}) async-start(bf16[16,4,64,512]{3,2,1,0:T(8,128)(2,1)} %bitcast.15), calls=%async_computation.1 | async-start | bytes 8388608 | tf_op jit(solution)/shard_map/all_to_all | solution.py:66
  149.6 92.2 %copy-start.1 = (f32[256]{0:T(256)S(1)}, f32[256]{0:T(256)}, u32[]{:S(2)}) copy-start(f32[256]{0:T(256)} %param.11) | copy-start | bytes 3076
  149.6 92.2 %copy-start.2 = (f32[256]{0:T(256)S(1)}, f32[256]{0:T(256)}, u32[]{:S(2)}) copy-start(f32[256]{0:T(256)} %param.12) | copy-start | bytes 3076
  149.6 92.2 %copy-start.3 = (f32[256]{0:T(256)S(1)}, f32[256]{0:T(256)}, u32[]{:S(2)}) copy-start(f32[256]{0:T(256)} %param.13) | copy-start | bytes 3076
  241.8 3.0 %copy-start = (bf16[3,3,3,512,256]{4,3,2,1,0:T(8,128)(2,1)S(1)}, bf16[3,3,3,512,256]{4,3,2,1,0:T(8,128)(2,1)}, u32[]{:S(2)}) copy-start(bf16[3,3,3,512,256]{4,3,2,1,0:T(8,128)(2,1)} %copy.13) | copy-start | bytes 21233668
